TPU v7x, 128 devices: a whole 4x4x4 slice. The times are simulated.
128 devices in a mesh: grid: 32 (over y, x, core), lev: 4 (over z).
Axes of the slice: x: 4, y: 4, z: 4, core: 2. Of those that a mesh axis runs over, the one named last changes fastest.
Arguments:
- trajectory: float32 [32, 1280, 4096], P('lev', 'grid'), may hold values from -6 to 6
- legendre: float32 [640, 1280, 640], P(('grid', 'lev')), as said below
- obs_cell: int32 [65536], P('grid'), may hold values from 0 to 40959, as said below
- obs_count: int32 [1024], P('grid'), may hold values from 0 to 64, as said below
- departure: float32 [65536, 128], P('grid'), may hold values from -6 to 6
- obs_weight: float32 [32, 65536], P('lev', 'grid'), may hold values from -6 to 6
- band_of: int32 [32], replicated, may hold values from 0 to 31, each once
- m_order: int32 [640], replicated, may hold values from 0 to 639, as said below
Outputs:
- spectral: float32 [640, 32, 2, 640], P(('grid', 'lev'))
Inputs may be any that keep to these rules, and one draw needn't show every extreme that they name: `obs_cell`: slots q * 64 to q * 64 + 63 of each device name blocks in rows q * 40 to q * 40 + 39. `obs_count`: some destination group receives 64 live slots from every device. `m_order`: each wavenumber once. legendre[j, l, n] is zero where n * 640 < m_order[j] * 640.
All inputs are finite; a program needn't handle non-finite values.
Results may differ from a plain program's by a relative error of at most 0.000098.
Values sent between devices are 32-bit elements; how exact they have to be, the bound alone decides.
No kernel may reach another device: no remote copies, remote signals or barrier semaphores. Data moves between devices by JAX's collectives and lax.ppermute only.
A program may use at most 128 MiB of HBM per device.

v0:
```python
import functools
import math

import jax
import jax.numpy as jnp
import numpy as np
from jax import lax
from jax.experimental import pallas as pl
from jax.experimental.pallas import tpu as pltpu
from jax.sharding import PartitionSpec as P

LANES = 128
SUB = 8
RADIX = 16
GROUPS = RADIX // 2
MIB = 1 << 20
F32 = jnp.float32
BF16 = jnp.bfloat16
I32 = jnp.int32


def wave_columns(wave_total):
    per_residue = wave_total // RADIX
    cols = np.zeros((GROUPS, 2 * per_residue), np.int32)
    for g in range(GROUPS):
        first, second = g, (RADIX - g if g else RADIX // 2)
        turns = RADIX * np.arange(per_residue)
        cols[g, :per_residue] = first + turns
        cols[g, per_residue : 2 * per_residue] = second + turns
    return cols


def wave_table(wave_total, lon_count):
    width = lon_count // RADIX
    cols = wave_columns(wave_total)
    per_residue = wave_total // RADIX
    fine = np.arange(width, dtype=np.int64)
    out = np.zeros((GROUPS, 2, width, 2, LANES), np.float64)
    for g in range(GROUPS):
        for i in range(2 * per_residue):
            m = int(cols[g, i])
            lane = (g * 2 * per_residue + i) % LANES
            angle = 2.0 * math.pi / lon_count * ((m * fine) % lon_count)
            factor = 1.0 if m == 0 else 2.0
            cos, sin = factor * np.cos(angle), factor * np.sin(angle)
            second = i >= per_residue
            if g == 0:
                part = 1 if second else 0
                out[g, part, :, 0, lane] = cos
                out[g, part, :, 1, lane] = -sin
            else:
                sign = -1.0 if second else 1.0
                out[g, 0, :, 0, lane] = cos
                out[g, 1, :, 0, lane] = sign * sin
                out[g, 0, :, 1, lane] = -sin
                out[g, 1, :, 1, lane] = sign * cos
    return out.reshape(GROUPS, 2 * width, 2 * LANES).astype(np.float32)


def split_np(table):
    high = table.astype(jnp.bfloat16)
    low = (table - high.astype(np.float32)).astype(jnp.bfloat16)
    return high, low


def split(x):
    high = x.astype(BF16)
    return high, (x - high.astype(F32)).astype(BF16)


def real_fft(xs):
    n = len(xs)
    if n == 2:
        return [(xs[0] + xs[1], None), (xs[0] - xs[1], None)]
    even, odd = real_fft(xs[0::2]), real_fft(xs[1::2])
    out = [None] * (n // 2 + 1)
    for k in range(n // 4 + 1):
        er, ei = even[k]
        orr, oi = odd[k]
        if k == 0:
            out[0] = (er + orr, None)
            out[n // 2] = (er - orr, None)
        elif 4 * k == n:
            out[k] = (er, -orr)
        else:
            c, s = math.cos(2 * math.pi * k / n), math.sin(2 * math.pi * k / n)
            if 8 * k == n:
                tr, ti = (orr + oi) * c, (oi - orr) * c
            else:
                tr, ti = orr * c + oi * s, oi * c - orr * s
            out[k] = (er + tr, ei + ti)
            out[n // 2 - k] = (er - tr, ti - ei)
    return out


def pack_kernel(
    capacity, cells_per_dev, count_hbm, dep_hbm, weight_hbm, cell_hbm, out_ref,
    counts, weights, cells_v, sems,
):
    groups = out_ref.shape[0]
    small = [
        pltpu.make_async_copy(src, dst, sems.at[i])
        for i, (src, dst) in enumerate(
            ((count_hbm, counts), (weight_hbm, weights), (cell_hbm, cells_v))
        )
    ]
    for copy in small:
        copy.start()
    parts = 4
    each = groups // parts
    large = [
        pltpu.make_async_copy(
            dep_hbm.at[pl.ds(i * each, each)],
            out_ref.at[pl.ds(i * each, each), pl.ds(0, capacity)],
            sems.at[3 + i],
        )
        for i in range(parts)
    ]
    for copy in large:
        copy.start()
    for copy in small:
        copy.wait()
    lane = lax.broadcasted_iota(I32, (SUB, LANES), 1)
    for q in range(groups):
        tile = q // 2
        weight = weights[:, tile * LANES : (tile + 1) * LANES]
        cells = jnp.broadcast_to(cells_v[tile : tile + 1, :], (SUB, LANES))
        cells = (cells - q * cells_per_dev).astype(F32)
        if q % 2:
            weight = pltpu.roll(weight, capacity, 1)
        else:
            cells = pltpu.roll(cells, capacity, 1)
        live = jnp.where(lane < counts[q], 1.0, 0.0)
        out_ref[q, capacity:, :] = jnp.where(lane < capacity, weight * live, cells)
    for copy in large:
        copy.wait()


def pack(obs_count, departure, obs_weight, obs_cell, cells_per_dev):
    groups = obs_count.shape[0]
    slots = departure.shape[0]
    capacity = slots // groups
    assert 2 * capacity == LANES and obs_weight.shape[0] == SUB
    cell_rows = obs_cell.reshape(slots // LANES, LANES)
    return pl.pallas_call(
        functools.partial(pack_kernel, capacity, cells_per_dev),
        out_shape=jax.ShapeDtypeStruct((groups, capacity + SUB, LANES), F32),
        in_specs=[pl.BlockSpec(memory_space=pltpu.HBM)] * 4,
        out_specs=pl.BlockSpec(memory_space=pltpu.VMEM),
        scratch_shapes=[
            pltpu.SMEM(obs_count.shape, I32),
            pltpu.VMEM(obs_weight.shape, F32),
            pltpu.VMEM(cell_rows.shape, I32),
            pltpu.SemaphoreType.DMA((7,)),
        ],
        compiler_params=pltpu.CompilerParams(vmem_limit_bytes=60 * MIB),
        name="pack",
    )(obs_count, departure.reshape(groups, capacity, LANES), obs_weight, cell_rows)


STREAMS = 4


def grid_kernel(
    recv_hbm, gain_hbm, thi_hbm, tlo_hbm, pick_hbm, out_hbm, *scratch
):
    acc = scratch[:STREAMS]
    (recv, extra, gain, thi, tlo, pick, cells_v, cells_s, wide, yhi, ylo, zt, out, sems) = scratch[
        STREAMS:
    ]
    groups, capacity, _ = recv.shape
    lat_dev = gain.shape[0]
    blocks = gain.shape[2] // LANES
    first = pltpu.make_async_copy(recv_hbm.at[:, pl.ds(capacity, SUB)], extra, sems.at[0])
    first.start()
    parts = 4
    each = groups // parts
    deps = [
        pltpu.make_async_copy(
            recv_hbm.at[pl.ds(i * each, each), pl.ds(0, capacity)],
            recv.at[pl.ds(i * each, each)],
            sems.at[2 + i],
        )
        for i in range(parts)
    ]
    half = lat_dev // 2
    loads = [
        pltpu.make_async_copy(src, dst, sems.at[2 + parts + i])
        for i, (src, dst) in enumerate(
            (
                (gain_hbm.at[pl.ds(0, half)], gain.at[pl.ds(0, half)]),
                (gain_hbm.at[pl.ds(half, half)], gain.at[pl.ds(half, half)]),
                (thi_hbm, thi),
                (tlo_hbm, tlo),
                (pick_hbm, pick),
            )
        )
    ]
    for copy in deps:
        copy.start()

    def clear(i, carry):
        for a in acc:
            a[pl.ds(i * SUB, SUB)] = jnp.zeros((SUB, SUB, LANES), F32)
        return carry

    lax.fori_loop(0, acc[0].shape[0] // SUB, clear, 0)

    first.wait()
    cells_v[...] = extra[:, 0, :].astype(I32)
    cell_copy = pltpu.make_async_copy(cells_v, cells_s, sems.at[1])
    cell_copy.start()

    rows = groups * SUB
    weight = extra[...].reshape(rows, LANES)
    lane = lax.broadcasted_iota(I32, (rows, LANES), 1)
    whi, wlo = split(weight)
    both = jnp.where(
        lane < capacity, whi.astype(F32), pltpu.roll(wlo.astype(F32), capacity, 1)
    ).astype(BF16)
    row = lax.broadcasted_iota(I32, (LANES, 2 * LANES), 0) % capacity
    col = lax.broadcasted_iota(I32, (LANES, 2 * LANES), 1) // LANES
    offset = row - col

    def widen(i, carry):
        ones = jnp.where(offset == 2 * i, 1.0, 0.0).astype(BF16)
        res = jnp.dot(both, ones, preferred_element_type=F32)
        wide[2 * i] = res[:, :LANES]
        wide[2 * i + 1] = res[:, LANES:]
        return carry

    lax.fori_loop(0, capacity // 2, widen, 0, unroll=4)
    cell_copy.wait()

    for copy in deps:
        copy.wait()
    for copy in loads:
        copy.start()

    def scatter(s, carry):
        w_rows = pl.ds(pl.multiple_of(s * SUB, SUB), SUB)
        for i in range(0, capacity, STREAMS):
            cells = [cells_s[s, capacity + i + t] for t in range(STREAMS)]
            old = [acc[t][cells[t]] for t in range(STREAMS)]
            new = []
            for t in range(STREAMS):
                k = i + t
                new.append(old[t] + wide[k, w_rows, :] * recv[s, k : k + 1, :])
            for t in range(STREAMS):
                acc[t][cells[t]] = new[t]
        return carry

    lax.fori_loop(0, groups, scatter, 0)
    for copy in loads[:2]:
        copy.wait()

    width = blocks // RADIX * LANES
    pair = 2

    def transform(i, carry):
        r0 = i * pair
        for h in range(blocks // RADIX):
            xs = []
            for a in range(RADIX):
                b = a * (blocks // RADIX) + h
                parts = []
                for r in range(pair):
                    cell = (r0 + r) * blocks + b
                    total = acc[0][cell]
                    for t in range(1, STREAMS):
                        total = total + acc[t][cell]
                    parts.append(total * gain[r0 + r, :, b * LANES : (b + 1) * LANES])
                xs.append(jnp.concatenate(parts, axis=0))
            ys = real_fft(xs)
            rows = pl.ds(pl.multiple_of(r0 * SUB, pair * SUB), pair * SUB)
            for g in range(GROUPS):
                re, im = ys[g] if g else (ys[0][0], ys[RADIX // 2][0])
                for part, value in enumerate((re, im)):
                    lanes = pl.ds(part * width + h * LANES, LANES)
                    hi, lo = split(value)
                    yhi[g, rows, lanes] = hi
                    ylo[g, rows, lanes] = lo
        return carry

    lax.fori_loop(0, lat_dev // pair, transform, 0)
    for copy in loads[2:]:
        copy.wait()

    def dot(a, b):
        return jnp.dot(a, b, preferred_element_type=F32)

    waves = pick.shape[0]
    members = waves // GROUPS
    lane = lax.broadcasted_iota(I32, (2 * lat_dev * SUB, LANES), 1)
    open_tile = None
    for g in range(GROUPS):
        high = yhi[g]
        z = dot(high, thi[g]) + (dot(high, tlo[g]) + dot(ylo[g], thi[g]))
        re = z[:, :LANES].reshape(lat_dev, 1, SUB, LANES)
        im = z[:, LANES:].reshape(lat_dev, 1, SUB, LANES)
        both = jnp.concatenate([re, im], axis=1).reshape(lat_dev * 2 * SUB, LANES)
        tile, offset = divmod(g * members, LANES)
        past = offset + members - LANES
        mine = jnp.where(lane >= offset, both, 0.0) if past > 0 else both
        open_tile = mine if open_tile is None else open_tile + mine
        if past >= 0:
            hi, lo = split(open_tile.T)
            zt[tile * LANES : (tile + 1) * LANES, :] = hi
            zt[waves + tile * LANES : waves + (tile + 1) * LANES, :] = lo
            open_tile = jnp.where(lane < past, both, 0.0) if past > 0 else None

    chunks = zt.shape[1] // LANES
    tall = LANES
    sends = []
    for j0 in range(0, waves, tall):
        sel = pick[j0 : j0 + tall, :]
        res = dot(jnp.concatenate([sel, sel], axis=1), zt[...])
        for jt in range(tall // SUB):
            for c in range(chunks):
                start = (j0 + jt * SUB) * chunks + c
                out[pl.ds(start, SUB, stride=chunks), :] = res[
                    jt * SUB : (jt + 1) * SUB, c * LANES : (c + 1) * LANES
                ]
        span = pl.ds(j0 * chunks, tall * chunks)
        sends.append(
            pltpu.make_async_copy(out.at[span], out_hbm.at[span], sems.at[11 + j0 // tall])
        )
        sends[-1].start()
    for copy in sends:
        copy.wait()


def grid_to_waves(recv, gain, thi, tlo, pick):
    lat_dev, ch_dev, lon_count = gain.shape
    waves = pick.shape[0]
    groups, capacity = recv.shape[0], recv.shape[1] - SUB
    cells = lat_dev * lon_count // LANES
    rows = lat_dev * ch_dev
    return pl.pallas_call(
        grid_kernel,
        out_shape=jax.ShapeDtypeStruct((waves * 2 * rows // LANES, LANES), F32),
        in_specs=[pl.BlockSpec(memory_space=pltpu.HBM)] * 5,
        out_specs=pl.BlockSpec(memory_space=pltpu.HBM),
        scratch_shapes=[pltpu.VMEM((cells, ch_dev, LANES), F32) for _ in range(STREAMS)]
        + [
            pltpu.VMEM((groups, capacity, LANES), F32),
            pltpu.VMEM((groups, SUB, LANES), F32),
            pltpu.VMEM(gain.shape, F32),
            pltpu.VMEM(thi.shape, BF16),
            pltpu.VMEM(tlo.shape, BF16),
            pltpu.VMEM(pick.shape, BF16),
            pltpu.VMEM((groups, LANES), I32),
            pltpu.SMEM((groups, LANES), I32),
            pltpu.VMEM((capacity, groups * SUB, LANES), F32),
            pltpu.VMEM((GROUPS, rows, thi.shape[1]), BF16),
            pltpu.VMEM((GROUPS, rows, thi.shape[1]), BF16),
            pltpu.VMEM((2 * waves, 2 * rows), BF16),
            pltpu.VMEM((waves * 2 * rows // LANES, LANES), F32),
            pltpu.SemaphoreType.DMA((11 + waves // LANES,)),
        ],
        compiler_params=pltpu.CompilerParams(vmem_limit_bytes=60 * MIB),
        name="grid_to_waves",
    )(recv, gain, thi, tlo, pick)


def prepare_kernel(lat_dev, band_ref, table_ref, hi_ref, lo_ref):
    grid_count = band_ref.shape[0]
    chunks = lat_dev // SUB
    half = 2 * SUB

    def body(c, carry):
        starts = [
            pl.multiple_of(band_ref[g] * lat_dev + c * SUB, SUB) for g in range(grid_count)
        ]
        for t in range(table_ref.shape[2] // LANES):
            lanes = pl.ds(t * LANES, LANES)
            for g0 in range(0, grid_count, half):
                turned = []
                for g1 in range(g0, g0 + half, SUB):
                    tiles = [
                        table_ref[0, pl.ds(starts[g], SUB), lanes] for g in range(g1, g1 + SUB)
                    ]
                    turned.append(jnp.swapaxes(jnp.stack(tiles), 0, 1))
                for k in range(SUB):
                    hi, lo = split(jnp.concatenate([x[k] for x in turned], axis=0))
                    start = pl.multiple_of((k * chunks + c) * grid_count + g0, half)
                    hi_ref[0, pl.ds(start, half), lanes] = hi
                    lo_ref[0, pl.ds(start, half), lanes] = lo
        return carry

    lax.fori_loop(0, chunks, body, 0)


def prepare_table(legendre, band_of, lat_dev):
    slot_count, lat_total, total_count = legendre.shape
    block = pl.BlockSpec((1, lat_total, total_count), lambda s: (s, 0, 0))
    return pl.pallas_call(
        functools.partial(prepare_kernel, lat_dev),
        grid=(slot_count,),
        out_shape=[jax.ShapeDtypeStruct(legendre.shape, BF16)] * 2,
        in_specs=[pl.BlockSpec(memory_space=pltpu.SMEM), block],
        out_specs=[block, block],
        compiler_params=pltpu.CompilerParams(vmem_limit_bytes=56 * MIB),
        cost_estimate=pl.CostEstimate(
            flops=4 * legendre.size, bytes_accessed=8 * legendre.size, transcendentals=0
        ),
        name="prepare_table",
    )(band_of, legendre)


def legendre_kernel(geo, x_hbm, lhi_hbm, llo_hbm, out_hbm, x_ref, lhi, llo, out, sems):
    grid_count, lev_count, slot_count, chunks = geo
    depth = chunks * grid_count
    wide = 2 * SUB
    first = pltpu.make_async_copy(x_hbm, x_ref, sems.at[0])
    first.start()

    def loads(slot):
        return [
            pltpu.make_async_copy(src.at[slot], dst.at[slot], sems.at[1 + 2 * slot + i])
            for i, (src, dst) in enumerate(((lhi_hbm, lhi), (llo_hbm, llo)))
        ]

    for slot in range(slot_count):
        for copy in loads(slot):
            copy.start()
    first.wait()

    def store(slot):
        return pltpu.make_async_copy(
            out.at[slot], out_hbm.at[slot], sems.at[1 + 2 * slot_count + slot]
        )

    def body(slot, carry):
        lhs = []
        for lev in range(lev_count):
            pieces = []
            for c in range(chunks):
                start = (lev * slot_count + slot) * chunks + c
                pieces.append(
                    x_ref[pl.ds(start, grid_count, stride=lev_count * slot_count * chunks), :]
                )
            lhs.append(jnp.concatenate(pieces, axis=0).T)
        for copy in loads(slot):
            copy.wait()
        total = None
        for k in range(LANES // wide):
            part = jnp.concatenate([m[k * wide : (k + 1) * wide] for m in lhs], axis=0)
            hi, lo = split(part)
            both = jnp.concatenate([hi, lo], axis=0)
            rows = pl.ds(k * depth, depth)
            prod = jnp.dot(both, lhi[slot, rows, :], preferred_element_type=F32)
            prod = prod[: hi.shape[0]] + (
                prod[hi.shape[0] :]
                + jnp.dot(hi, llo[slot, rows, :], preferred_element_type=F32)
            )
            total = prod if total is None else total + prod
        for lev in range(lev_count):
            re = total[lev * wide : lev * wide + SUB]
            im = total[lev * wide + SUB : (lev + 1) * wide]
            out[slot, lev * SUB : (lev + 1) * SUB] = jnp.stack([re, im], axis=1)
        store(slot).start()
        return carry

    lax.fori_loop(0, slot_count, body, 0)
    for slot in range(slot_count):
        store(slot).wait()


def legendre_step(waves, lhi, llo, grid_count, lev_count):
    slot_count, lat_total, total_count = lhi.shape
    chunks = waves.shape[0] // (grid_count * lev_count * slot_count)
    geo = (grid_count, lev_count, slot_count, chunks)
    out_shape = (slot_count, lev_count * SUB, 2, total_count)
    return pl.pallas_call(
        functools.partial(legendre_kernel, geo),
        out_shape=jax.ShapeDtypeStruct(out_shape, F32),
        in_specs=[pl.BlockSpec(memory_space=pltpu.HBM)] * 3,
        out_specs=pl.BlockSpec(memory_space=pltpu.HBM),
        scratch_shapes=[
            pltpu.VMEM(waves.shape, F32),
            pltpu.VMEM(lhi.shape, BF16),
            pltpu.VMEM(llo.shape, BF16),
            pltpu.VMEM(out_shape, F32),
            pltpu.SemaphoreType.DMA((1 + 3 * slot_count,)),
        ],
        compiler_params=pltpu.CompilerParams(vmem_limit_bytes=60 * MIB),
        name="legendre_step",
    )(waves, lhi, llo)


def shards(trajectory, legendre, obs_cell, obs_count, departure, obs_weight, band_of, m_order):
    grid_count = lax.axis_size("grid")
    lev_count = lax.axis_size("lev")
    ch_dev, lat_dev, lon_count = trajectory.shape
    slot_count, lat_total, total_count = legendre.shape
    wave_total = m_order.shape[0]
    cells_per_dev = lat_dev * lon_count // LANES

    sent = pack(obs_count, departure, obs_weight, obs_cell, cells_per_dev)
    recv = lax.all_to_all(sent, "grid", split_axis=0, concat_axis=0, tiled=True)

    gain = jnp.swapaxes(1.0 + 0.5 * jnp.tanh(trajectory), 0, 1)
    thi, tlo = split_np(wave_table(wave_total, lon_count))
    cols = wave_columns(wave_total).reshape(1, -1)
    pick = (m_order[:, None] == cols).astype(BF16)

    waves = grid_to_waves(recv, gain, jnp.asarray(thi), jnp.asarray(tlo), pick)
    outgoing = waves.reshape(grid_count * lev_count, 1, -1)
    incoming = lax.all_to_all(
        outgoing, ("grid", "lev"), split_axis=0, concat_axis=0, tiled=True
    )

    lhi, llo = prepare_table(legendre, band_of, lat_dev)
    return legendre_step(
        incoming.reshape(-1, LANES), lhi, llo, grid_count, lev_count
    )


def solution(mesh):
    placed = (
        P("lev", "grid", None),
        P(("grid", "lev"), None, None),
        P("grid"),
        P("grid"),
        P("grid", None),
        P("lev", "grid"),
        P(),
        P(),
    )
    return jax.shard_map(
        shards,
        mesh=mesh,
        in_specs=placed,
        out_specs=P(("grid", "lev"), None, None, None),
        check_vma=False,
    )
```

profile of v0, /device:TPU:1, one launch (start us, length us, event | category | flops | bytes accessed | tf_op | source)
XLA Modules:
  0.0 87.1 jit_solution(8707046297257074017)
XLA Ops:
  0.0 2.4 %pack.1 = f32[32,72,128]{2,1,0:T(8,128)} custom-call(s32[32]{0:T(128)} %count_hbm.1, f32[32,64,128]{2,1,0:T(8,128)} %bitcast.8, f32[8,2048]{1,0:T(8,128)} %weight_hbm.1, s32[16,128]{1,0:T(8,128)} %bitcast.9), custom_call_target="tpu_custom_call" | custom-call | tf_op jit(solution)/shard_map/pack/pallas_call | solution.py:145
  2.4 8.6 %all-to-all-start = ((f32[32,72,128]{2,1,0:T(8,128)}), f32[32,72,128]{2,1,0:T(8,128)S(1)}, u32[]{:S(2)}, u32[]{:S(2)}) async-start(f32[32,72,128]{2,1,0:T(8,128)} %pack.1), calls=%async_computation | async-start | bytes 2359296 | tf_op jit(solution)/shard_map/all_to_all | solution.py:501
  11.0 1.8 %compare_convert_fusion.pick_hbm = bf16[640,640]{1,0:T(8,128)(2,1)} fusion(s32[640]{0:T(1024)} %constant.15, s32[640]{0:T(1024)} %param.18), kind=kLoop, calls=%fused_computation.4 | loop fusion | flops 819200 | bytes 824320 | tf_op jit(solution)/shard_map/convert_element_type | solution.py:506
  12.8 8.4 %fusion.2.gain_hbm = f32[40,8,4096]{2,1,0:T(8,128)} fusion(f32[8,40,4096]{2,1,0:T(8,128)} %param.11), kind=kLoop, calls=%fused_computation.3 | loop fusion | flops 2621440 | bytes 10485760 | tf_op jit(solution)/shard_map/transpose | solution.py:503
  21.2 7.5 %all-to-all-done.recv_hbm = f32[32,72,128]{2,1,0:T(8,128)S(1)} async-done(((f32[32,72,128]{2,1,0:T(8,128)}), f32[32,72,128]{2,1,0:T(8,128)S(1)}, u32[]{:S(2)}, u32[]{:S(2)}) %all-to-all-start) | async-done | bytes 1179680 | tf_op jit(solution)/shard_map/all_to_all | solution.py:501
  28.7 0.0 copy-start.1
  28.7 1.1 %copy-done.1 = f32[32,72,128]{2,1,0:T(8,128)} copy-done((f32[32,72,128]{2,1,0:T(8,128)}, f32[32,72,128]{2,1,0:T(8,128)S(1)}, u32[]{:S(2)}) %copy-start.1) | copy-done | bytes 1179672
  29.7 14.4 %grid_to_waves.1 = f32[3200,128]{1,0:T(8,128)} custom-call(f32[32,72,128]{2,1,0:T(8,128)} %copy-done.1, f32[40,8,4096]{2,1,0:T(8,128)} %fusion.2.gain_hbm, bf16[8,512,256]{2,1,0:T(8,128)(2,1)} %constant.11.clone.thi_hbm, bf16[8,512,256]{2,1,0:T(8,128)(2,1)} %constant.12.clone.tlo_hbm, bf16[640,640]{1,0:T(8,128)(2,1)} %compare_convert_fusion.pick_hbm), custom_call_target="tpu_custom_call" | custom-call | tf_op jit(solution)/shard_map/grid_to_waves/pallas_call | solution.py:339
  44.1 7.5 %all-to-all-start.1 = ((f32[128,1,3200]{2,1,0:T(1,128)}), f32[128,1,3200]{2,1,0:T(1,128)S(1)}, u32[]{:S(2)}, u32[]{:S(2)}) async-start(f32[128,1,3200]{2,1,0:T(1,128)} %bitcast.7), calls=%async_computation.1 | async-start | bytes 3276800 | tf_op jit(solution)/shard_map/all_to_all | solution.py:510
  51.6 15.7 %prepare_table.1 = (bf16[5,1280,640]{2,1,0:T(8,128)(2,1)}, bf16[5,1280,640]{2,1,0:T(8,128)(2,1)}) custom-call(s32[32]{0:T(128)} %band_ref.1, f32[5,1280,640]{2,1,0:T(8,128)} %table_ref.1), custom_call_target="tpu_custom_call" | custom-call | flops 16384000 | bytes 32768000 | tf_op jit(solution)/shard_map/prepare_table/pallas_call | solution.py:397
  67.4 9.9 %all-to-all-done.1 = f32[128,1,3200]{2,1,0:T(1,128)S(1)} async-done(((f32[128,1,3200]{2,1,0:T(1,128)}), f32[128,1,3200]{2,1,0:T(1,128)S(1)}, u32[]{:S(2)}, u32[]{:S(2)}) %all-to-all-start.1) | async-done | bytes 1638432 | tf_op jit(solution)/shard_map/all_to_all | solution.py:510
  77.3 0.0 copy-start
  77.3 1.2 %copy-done = f32[128,1,3200]{2,1,0:T(1,128)} copy-done((f32[128,1,3200]{2,1,0:T(1,128)}, f32[128,1,3200]{2,1,0:T(1,128)S(1)}, u32[]{:S(2)}) %copy-start) | copy-done | bytes 1638424
  78.4 8.7 %legendre_step.1 = f32[5,32,2,640]{3,2,1,0:T(2,128)} custom-call(f32[3200,128]{1,0:T(8,128)} %bitcast.6, bf16[5,1280,640]{2,1,0:T(8,128)(2,1)} %get-tuple-element.7.lhi_hbm, bf16[5,1280,640]{2,1,0:T(8,128)(2,1)} %get-tuple-element.8.llo_hbm), custom_call_target="tpu_custom_call" | custom-call | tf_op jit(solution)/shard_map/legendre_step/pallas_call | solution.py:475
Async XLA Ops:
  2.4 26.3 %all-to-all-start = ((f32[32,72,128]{2,1,0:T(8,128)}), f32[32,72,128]{2,1,0:T(8,128)S(1)}, u32[]{:S(2)}, u32[]{:S(2)}) async-start(f32[32,72,128]{2,1,0:T(8,128)} %pack.1), calls=%async_computation | async-start | bytes 2359296 | tf_op jit(solution)/shard_map/all_to_all | solution.py:501
  28.7 1.1 %copy-start.1 = (f32[32,72,128]{2,1,0:T(8,128)}, f32[32,72,128]{2,1,0:T(8,128)S(1)}, u32[]{:S(2)}) copy-start(f32[32,72,128]{2,1,0:T(8,128)S(1)} %all-to-all-done.recv_hbm) | copy-start | bytes 3538948
  44.1 33.2 %all-to-all-start.1 = ((f32[128,1,3200]{2,1,0:T(1,128)}), f32[128,1,3200]{2,1,0:T(1,128)S(1)}, u32[]{:S(2)}, u32[]{:S(2)}) async-start(f32[128,1,3200]{2,1,0:T(1,128)} %bitcast.7), calls=%async_computation.1 | async-start | bytes 3276800 | tf_op jit(solution)/shard_map/all_to_all | solution.py:510
  77.3 1.2 %copy-start = (f32[128,1,3200]{2,1,0:T(1,128)}, f32[128,1,3200]{2,1,0:T(1,128)S(1)}, u32[]{:S(2)}) copy-start(f32[128,1,3200]{2,1,0:T(1,128)S(1)} %all-to-all-done.1) | copy-start | bytes 4915204
where the time goes:
time: 87.6 us; the launch traced here: 87.1 us
  Pallas kernels  41.1 us (47%)
  waiting for transfers between devices  17.4 us (20%)
  starting transfers between devices  16.1 us (18%)
  other arithmetic  10.2 us (12%)
  local copies, waits for them, and re-layouts  2.22 us (3%)
    pallas_call x1, Pallas kernels, prepare_table(): pl.pallas_call(functools.partial(prepare_kernel, lat_dev), grid=(slot_cou...  15.7 us
    pallas_call x1, Pallas kernels, grid_to_waves(): pl.pallas_call(grid_kernel, out_shape=jax.ShapeDtypeStruct((waves * 2 * r...  14.4 us
    all_to_all x1, waiting for transfers between devices, shards(): lax.all_to_all(outgoing, ('grid', 'lev'), split_axis=0, concat_axis=0, ti...  9.91 us
    pallas_call x1, Pallas kernels, legendre_step(): pl.pallas_call(functools.partial(legendre_kernel, geo), out_shape=jax.Sha...  8.66 us
    all_to_all x1, starting transfers between devices, shards(): recv = lax.all_to_all(sent, 'grid', split_axis=0, concat_axis=0, tiled=True)  8.6 us
    transpose x1, other arithmetic, shards(): gain = jnp.swapaxes(1.0 + 0.5 * jnp.tanh(trajectory), 0, 1)  8.39 us
    all_to_all x1, starting transfers between devices, shards(): lax.all_to_all(outgoing, ('grid', 'lev'), split_axis=0, concat_axis=0, ti...  7.53 us
    all_to_all x1, waiting for transfers between devices, shards(): recv = lax.all_to_all(sent, 'grid', split_axis=0, concat_axis=0, tiled=True)  7.49 us
  transfers between devices with their start and end apart: 2, of which 2 were waited for; matrix products, arithmetic and copies ran while one was open for 12% of the time, Pallas kernels for 18%

commit v1 on v0

--- a/solution.py
+++ b/solution.py
@@ -159,13 +159,14 @@
 
 
 STREAMS = 4
+AHEAD = 5
 
 
 def grid_kernel(
     recv_hbm, gain_hbm, thi_hbm, tlo_hbm, pick_hbm, out_hbm, *scratch
 ):
     acc = scratch[:STREAMS]
-    (recv, extra, gain, thi, tlo, pick, cells_v, cells_s, wide, yhi, ylo, zt, out, sems) = scratch[
+    (recv, extra, gain, thi, tlo, pick, cells_v, cells_s, wide_a, wide_b, yhi, ylo, zt, out, sems) = scratch[
         STREAMS:
     ]
     groups, capacity, _ = recv.shape
@@ -222,35 +223,39 @@
     col = lax.broadcasted_iota(I32, (LANES, 2 * LANES), 1) // LANES
     offset = row - col
 
-    def widen(i, carry):
-        ones = jnp.where(offset == 2 * i, 1.0, 0.0).astype(BF16)
-        res = jnp.dot(both, ones, preferred_element_type=F32)
-        wide[2 * i] = res[:, :LANES]
-        wide[2 * i + 1] = res[:, LANES:]
-        return carry
-
-    lax.fori_loop(0, capacity // 2, widen, 0, unroll=4)
+    def widen(ref, k0):
+        ones = jnp.where(offset == k0, 1.0, 0.0).astype(BF16)
+        ref[...] = jnp.dot(both, ones, preferred_element_type=F32)
+
+    def add_slots(ref, k0):
+        per = STREAMS // 2
+        for s0 in range(0, groups, per):
+            slots = [(s0 + t // 2, t % 2) for t in range(STREAMS)]
+            cells = [cells_s[s, capacity + k0 + kk] for s, kk in slots]
+            old = [acc[t][cells[t]] for t in range(STREAMS)]
+            new = []
+            for t, (s, kk) in enumerate(slots):
+                weights = ref[s * SUB : (s + 1) * SUB, kk * LANES : (kk + 1) * LANES]
+                new.append(old[t] + weights * recv[s, pl.ds(k0 + kk, 1), :])
+            for t in range(STREAMS):
+                acc[t][cells[t]] = new[t]
+
+    widen(wide_a, 0)
     cell_copy.wait()
-
     for copy in deps:
         copy.wait()
     for copy in loads:
         copy.start()
 
-    def scatter(s, carry):
-        w_rows = pl.ds(pl.multiple_of(s * SUB, SUB), SUB)
-        for i in range(0, capacity, STREAMS):
-            cells = [cells_s[s, capacity + i + t] for t in range(STREAMS)]
-            old = [acc[t][cells[t]] for t in range(STREAMS)]
-            new = []
-            for t in range(STREAMS):
-                k = i + t
-                new.append(old[t] + wide[k, w_rows, :] * recv[s, k : k + 1, :])
-            for t in range(STREAMS):
-                acc[t][cells[t]] = new[t]
+    def scatter(i, carry):
+        k0 = 4 * i
+        widen(wide_b, k0 + 2)
+        add_slots(wide_a, k0)
+        widen(wide_a, k0 + 4)
+        add_slots(wide_b, k0 + 2)
         return carry
 
-    lax.fori_loop(0, groups, scatter, 0)
+    lax.fori_loop(0, capacity // 4, scatter, 0)
     for copy in loads[:2]:
         copy.wait()
 
@@ -294,8 +299,11 @@
     lane = lax.broadcasted_iota(I32, (2 * lat_dev * SUB, LANES), 1)
     open_tile = None
     for g in range(GROUPS):
-        high = yhi[g]
-        z = dot(high, thi[g]) + (dot(high, tlo[g]) + dot(ylo[g], thi[g]))
+        high, top = yhi[g], thi[g]
+        z = dot(
+            jnp.concatenate([high, high, ylo[g]], axis=1),
+            jnp.concatenate([top, tlo[g], top], axis=0),
+        )
         re = z[:, :LANES].reshape(lat_dev, 1, SUB, LANES)
         im = z[:, LANES:].reshape(lat_dev, 1, SUB, LANES)
         both = jnp.concatenate([re, im], axis=1).reshape(lat_dev * 2 * SUB, LANES)
@@ -351,14 +359,15 @@
             pltpu.VMEM(pick.shape, BF16),
             pltpu.VMEM((groups, LANES), I32),
             pltpu.SMEM((groups, LANES), I32),
-            pltpu.VMEM((capacity, groups * SUB, LANES), F32),
+            pltpu.VMEM((groups * SUB, 2 * LANES), F32),
+            pltpu.VMEM((groups * SUB, 2 * LANES), F32),
             pltpu.VMEM((GROUPS, rows, thi.shape[1]), BF16),
             pltpu.VMEM((GROUPS, rows, thi.shape[1]), BF16),
             pltpu.VMEM((2 * waves, 2 * rows), BF16),
             pltpu.VMEM((waves * 2 * rows // LANES, LANES), F32),
             pltpu.SemaphoreType.DMA((11 + waves // LANES,)),
         ],
-        compiler_params=pltpu.CompilerParams(vmem_limit_bytes=60 * MIB),
+        compiler_params=pltpu.CompilerParams(vmem_limit_bytes=52 * MIB),
         name="grid_to_waves",
     )(recv, gain, thi, tlo, pick)
 
@@ -366,6 +375,8 @@
 def prepare_kernel(lat_dev, band_ref, table_ref, hi_ref, lo_ref):
     grid_count = band_ref.shape[0]
     chunks = lat_dev // SUB
+    full = LANES // grid_count
+    assert chunks == full + 1
     half = 2 * SUB
 
     def body(c, carry):
@@ -383,7 +394,10 @@
                     turned.append(jnp.swapaxes(jnp.stack(tiles), 0, 1))
                 for k in range(SUB):
                     hi, lo = split(jnp.concatenate([x[k] for x in turned], axis=0))
-                    start = pl.multiple_of((k * chunks + c) * grid_count + g0, half)
+                    start = jnp.where(
+                        c < full, k * LANES + c * grid_count, full * SUB * grid_count + k * grid_count
+                    )
+                    start = pl.multiple_of(start + g0, half)
                     hi_ref[0, pl.ds(start, half), lanes] = hi
                     lo_ref[0, pl.ds(start, half), lanes] = lo
         return carry
@@ -410,7 +424,7 @@
 
 def legendre_kernel(geo, x_hbm, lhi_hbm, llo_hbm, out_hbm, x_ref, lhi, llo, out, sems):
     grid_count, lev_count, slot_count, chunks = geo
-    depth = chunks * grid_count
+    full = LANES // grid_count
     wide = 2 * SUB
     first = pltpu.make_async_copy(x_hbm, x_ref, sems.at[0])
     first.start()
@@ -421,7 +435,7 @@
             for i, (src, dst) in enumerate(((lhi_hbm, lhi), (llo_hbm, llo)))
         ]
 
-    for slot in range(slot_count):
+    for slot in range(AHEAD):
         for copy in loads(slot):
             copy.start()
     first.wait()
@@ -443,18 +457,25 @@
             lhs.append(jnp.concatenate(pieces, axis=0).T)
         for copy in loads(slot):
             copy.wait()
-        total = None
-        for k in range(LANES // wide):
-            part = jnp.concatenate([m[k * wide : (k + 1) * wide] for m in lhs], axis=0)
-            hi, lo = split(part)
-            both = jnp.concatenate([hi, lo], axis=0)
-            rows = pl.ds(k * depth, depth)
-            prod = jnp.dot(both, lhi[slot, rows, :], preferred_element_type=F32)
-            prod = prod[: hi.shape[0]] + (
-                prod[hi.shape[0] :]
-                + jnp.dot(hi, llo[slot, rows, :], preferred_element_type=F32)
-            )
-            total = prod if total is None else total + prod
+
+        @pl.when(slot + AHEAD < slot_count)
+        def _():
+            for copy in loads(slot + AHEAD):
+                copy.start()
+
+        steps = range(LANES // wide)
+        cut = full * grid_count
+        main = [
+            jnp.concatenate([m[k * wide : (k + 1) * wide, :cut] for m in lhs], axis=0) for k in steps
+        ]
+        rest = [
+            jnp.concatenate([m[k * wide : (k + 1) * wide, cut:] for m in lhs], axis=0) for k in steps
+        ]
+        hi, lo = split(jnp.concatenate(main + rest, axis=1))
+        both = jnp.concatenate([hi, lo], axis=0)
+        prod = jnp.dot(both, lhi[slot], preferred_element_type=F32)
+        tail = jnp.dot(hi, llo[slot], preferred_element_type=F32)
+        total = prod[: hi.shape[0]] + (prod[hi.shape[0] :] + tail)
         for lev in range(lev_count):
             re = total[lev * wide : lev * wide + SUB]
             im = total[lev * wide + SUB : (lev + 1) * wide]
@@ -484,7 +505,7 @@
             pltpu.VMEM(out_shape, F32),
             pltpu.SemaphoreType.DMA((1 + 3 * slot_count,)),
         ],
-        compiler_params=pltpu.CompilerParams(vmem_limit_bytes=60 * MIB),
+        compiler_params=pltpu.CompilerParams(vmem_limit_bytes=50 * MIB),
         name="legendre_step",
     )(waves, lhi, llo)
 

time: 87.6 us -> 84.2 us (0.961)
  local copies, waits for them, and re-layouts: 2.22 us -> 0 us
  Pallas kernels: 41.1 us -> 40 us
  waiting for transfers between devices: 17.4 us -> 18.3 us
  other arithmetic: 10.2 us -> 9.3 us
    unnamed x4 -> x0, local copies, waits for them, and re-layouts: 2.22 us -> none
    pallas_call x1, Pallas kernels: 8.66 us -> 7.73 us  [legendre_step(): pl.pallas_call(functools.partial(legendre_kernel, geo), out_shape=jax.Sha...]
    all_to_all x1, waiting for transfers between devices: 7.49 us -> 8.38 us  [shards(): recv = lax.all_to_all(sent, 'grid', split_axis=0, concat_axis=0, tiled=True)]
    convert_element_type x1, other arithmetic: 1.8 us -> 0.91 us  [shards(): pick = (m_order[:, None] == cols).astype(BF16)]
  transfers between devices with their start and end apart: 2 -> 2, of which waited for: 2 -> 2; matrix products, arithmetic and copies ran while one was open for 12% -> 11% of each run, Pallas kernels for 18% -> 19%
where the time goes in v1:
time: 84.2 us; the launch traced here: 83.8 us
  Pallas kernels  40 us (48%)
  waiting for transfers between devices  18.3 us (22%)
  starting transfers between devices  16.1 us (19%)
  other arithmetic  9.3 us (11%)
    pallas_call x1, Pallas kernels, prepare_table(): pl.pallas_call(functools.partial(prepare_kernel, lat_dev), grid=(slot_cou...  15.7 us
    pallas_call x1, Pallas kernels, grid_to_waves(): pl.pallas_call(grid_kernel, out_shape=jax.ShapeDtypeStruct((waves * 2 * r...  14.2 us
    all_to_all x1, waiting for transfers between devices, shards(): lax.all_to_all(outgoing, ('grid', 'lev'), split_axis=0, concat_axis=0, ti...  9.89 us
    all_to_all x1, starting transfers between devices, shards(): recv = lax.all_to_all(sent, 'grid', split_axis=0, concat_axis=0, tiled=True)  8.6 us
    transpose x1, other arithmetic, shards(): gain = jnp.swapaxes(1.0 + 0.5 * jnp.tanh(trajectory), 0, 1)  8.39 us
    all_to_all x1, waiting for transfers between devices, shards(): recv = lax.all_to_all(sent, 'grid', split_axis=0, concat_axis=0, tiled=True)  8.38 us
    pallas_call x1, Pallas kernels, legendre_step(): pl.pallas_call(functools.partial(legendre_kernel, geo), out_shape=jax.Sha...  7.73 us
    all_to_all x1, starting transfers between devices, shards(): lax.all_to_all(outgoing, ('grid', 'lev'), split_axis=0, concat_axis=0, ti...  7.55 us
  transfers between devices with their start and end apart: 2, of which 2 were waited for; matrix products, arithmetic and copies ran while one was open for 11% of the time, Pallas kernels for 19%

profile of v1, /device:TPU:1, one launch (start us, length us, event | category | flops | bytes accessed | tf_op | source)
XLA Modules:
  0.0 83.8 jit_solution(11531801822963782035)
XLA Ops:
  0.0 2.3 %pack.1 = f32[32,72,128]{2,1,0:T(8,128)} custom-call(s32[32]{0:T(128)} %count_hbm.1, f32[32,64,128]{2,1,0:T(8,128)} %bitcast.8, f32[8,2048]{1,0:T(8,128)} %weight_hbm.1, s32[16,128]{1,0:T(8,128)} %bitcast.9), custom_call_target="tpu_custom_call" | custom-call | tf_op jit(solution)/shard_map/pack/pallas_call | solution.py:145
  2.3 8.6 %all-to-all-start = ((f32[32,72,128]{2,1,0:T(8,128)}), f32[32,72,128]{2,1,0:T(8,128)S(1)}, u32[]{:S(2)}, u32[]{:S(2)}) async-start(f32[32,72,128]{2,1,0:T(8,128)} %pack.1), calls=%async_computation | async-start | bytes 2359296 | tf_op jit(solution)/shard_map/all_to_all | solution.py:522
  10.9 0.9 %compare_convert_fusion.pick_hbm = bf16[640,640]{1,0:T(8,128)(2,1)S(1)} fusion(s32[640]{0:T(1024)} %constant.15, s32[640]{0:T(1024)} %param.18), kind=kLoop, calls=%fused_computation.4 | loop fusion | flops 819200 | bytes 824320 | tf_op jit(solution)/shard_map/convert_element_type | solution.py:527
  11.9 8.4 %fusion.2.gain_hbm = f32[40,8,4096]{2,1,0:T(8,128)} fusion(f32[8,40,4096]{2,1,0:T(8,128)} %param.11), kind=kLoop, calls=%fused_computation.3 | loop fusion | flops 2621440 | bytes 10485760 | tf_op jit(solution)/shard_map/transpose | solution.py:524
  20.3 8.4 %all-to-all-done.recv_hbm = f32[32,72,128]{2,1,0:T(8,128)S(1)} async-done(((f32[32,72,128]{2,1,0:T(8,128)}), f32[32,72,128]{2,1,0:T(8,128)S(1)}, u32[]{:S(2)}, u32[]{:S(2)}) %all-to-all-start) | async-done | bytes 1179680 | tf_op jit(solution)/shard_map/all_to_all | solution.py:522
  28.6 14.2 %grid_to_waves.1 = f32[3200,128]{1,0:T(8,128)} custom-call(f32[32,72,128]{2,1,0:T(8,128)S(1)} %all-to-all-done.recv_hbm, f32[40,8,4096]{2,1,0:T(8,128)} %fusion.2.gain_hbm, bf16[8,512,256]{2,1,0:T(8,128)(2,1)} %constant.11.clone.thi_hbm, bf16[8,512,256]{2,1,0:T(8,128)(2,1)} %constant.12.clone.tlo_hbm, bf16[640,640]{1,0:T(8,128)(2,1)S(1)} %compare_convert_fusion.pick_hbm), custom_call_target="tpu_custom_call" | custom-call | tf_op jit(solution)/shard_map/grid_to_waves/pallas_call | solution.py:347
  42.9 7.5 %all-to-all-start.1 = ((f32[128,1,3200]{2,1,0:T(1,128)}), f32[128,1,3200]{2,1,0:T(1,128)S(1)}, u32[]{:S(2)}, u32[]{:S(2)}) async-start(f32[128,1,3200]{2,1,0:T(1,128)} %bitcast.7), calls=%async_computation.1 | async-start | bytes 3276800 | tf_op jit(solution)/shard_map/all_to_all | solution.py:531
  50.4 15.7 %prepare_table.1 = (bf16[5,1280,640]{2,1,0:T(8,128)(2,1)}, bf16[5,1280,640]{2,1,0:T(8,128)(2,1)}) custom-call(s32[32]{0:T(128)} %band_ref.1, f32[5,1280,640]{2,1,0:T(8,128)} %table_ref.1), custom_call_target="tpu_custom_call" | custom-call | flops 16384000 | bytes 32768000 | tf_op jit(solution)/shard_map/prepare_table/pallas_call | solution.py:411
  66.2 9.9 %all-to-all-done.1 = f32[128,1,3200]{2,1,0:T(1,128)S(1)} async-done(((f32[128,1,3200]{2,1,0:T(1,128)}), f32[128,1,3200]{2,1,0:T(1,128)S(1)}, u32[]{:S(2)}, u32[]{:S(2)}) %all-to-all-start.1) | async-done | bytes 1638432 | tf_op jit(solution)/shard_map/all_to_all | solution.py:531
  76.1 7.7 %legendre_step.1 = f32[5,32,2,640]{3,2,1,0:T(2,128)} custom-call(f32[3200,128]{1,0:T(8,128)S(1)} %bitcast.6, bf16[5,1280,640]{2,1,0:T(8,128)(2,1)} %get-tuple-element.7.lhi_hbm, bf16[5,1280,640]{2,1,0:T(8,128)(2,1)} %get-tuple-element.8.llo_hbm), custom_call_target="tpu_custom_call" | custom-call | tf_op jit(solution)/shard_map/legendre_step/pallas_call | solution.py:496
Async XLA Ops:
  2.3 26.3 %all-to-all-start = ((f32[32,72,128]{2,1,0:T(8,128)}), f32[32,72,128]{2,1,0:T(8,128)S(1)}, u32[]{:S(2)}, u32[]{:S(2)}) async-start(f32[32,72,128]{2,1,0:T(8,128)} %pack.1), calls=%async_computation | async-start | bytes 2359296 | tf_op jit(solution)/shard_map/all_to_all | solution.py:522
  42.9 33.2 %all-to-all-start.1 = ((f32[128,1,3200]{2,1,0:T(1,128)}), f32[128,1,3200]{2,1,0:T(1,128)S(1)}, u32[]{:S(2)}, u32[]{:S(2)}) async-start(f32[128,1,3200]{2,1,0:T(1,128)} %bitcast.7), calls=%async_computation.1 | async-start | bytes 3276800 | tf_op jit(solution)/shard_map/all_to_all | solution.py:531

commit v2 on v1

--- a/solution.py
+++ b/solution.py
@@ -94,10 +94,10 @@
 
 
 def pack_kernel(
-    capacity, cells_per_dev, count_hbm, dep_hbm, weight_hbm, cell_hbm, out_ref,
-    counts, weights, cells_v, sems,
+    capacity, cells_per_dev, count_hbm, dep_hbm, weight_hbm, cell_hbm, out_hbm,
+    counts, weights, cells_v, out, sems,
 ):
-    groups = out_ref.shape[0]
+    groups = out.shape[0]
     small = [
         pltpu.make_async_copy(src, dst, sems.at[i])
         for i, (src, dst) in enumerate(
@@ -111,7 +111,7 @@
     large = [
         pltpu.make_async_copy(
             dep_hbm.at[pl.ds(i * each, each)],
-            out_ref.at[pl.ds(i * each, each), pl.ds(0, capacity)],
+            out.at[pl.ds(i * each, each), pl.ds(0, capacity)],
             sems.at[3 + i],
         )
         for i in range(parts)
@@ -131,8 +131,16 @@
         else:
             cells = pltpu.roll(cells, capacity, 1)
         live = jnp.where(lane < counts[q], 1.0, 0.0)
-        out_ref[q, capacity:, :] = jnp.where(lane < capacity, weight * live, cells)
-    for copy in large:
+        out[q, capacity:, :] = jnp.where(lane < capacity, weight * live, cells)
+    sends = []
+    for i in range(parts):
+        large[i].wait()
+        span = pl.ds(i * each, each)
+        sends.append(
+            pltpu.make_async_copy(out.at[span], out_hbm.at[span], sems.at[3 + parts + i])
+        )
+        sends[-1].start()
+    for copy in sends:
         copy.wait()
 
 
@@ -142,16 +150,18 @@
     capacity = slots // groups
     assert 2 * capacity == LANES and obs_weight.shape[0] == SUB
     cell_rows = obs_cell.reshape(slots // LANES, LANES)
+    out_shape = (groups, capacity + SUB, LANES)
     return pl.pallas_call(
         functools.partial(pack_kernel, capacity, cells_per_dev),
-        out_shape=jax.ShapeDtypeStruct((groups, capacity + SUB, LANES), F32),
+        out_shape=jax.ShapeDtypeStruct(out_shape, F32),
         in_specs=[pl.BlockSpec(memory_space=pltpu.HBM)] * 4,
-        out_specs=pl.BlockSpec(memory_space=pltpu.VMEM),
+        out_specs=pl.BlockSpec(memory_space=pltpu.HBM),
         scratch_shapes=[
             pltpu.SMEM(obs_count.shape, I32),
             pltpu.VMEM(obs_weight.shape, F32),
             pltpu.VMEM(cell_rows.shape, I32),
-            pltpu.SemaphoreType.DMA((7,)),
+            pltpu.VMEM(out_shape, F32),
+            pltpu.SemaphoreType.DMA((11,)),
         ],
         compiler_params=pltpu.CompilerParams(vmem_limit_bytes=60 * MIB),
         name="pack",
@@ -163,30 +173,19 @@
 
 
 def grid_kernel(
-    recv_hbm, gain_hbm, thi_hbm, tlo_hbm, pick_hbm, out_hbm, *scratch
+    recv, gain_hbm, thi_hbm, tlo_hbm, pick_hbm, out_hbm, *scratch
 ):
     acc = scratch[:STREAMS]
-    (recv, extra, gain, thi, tlo, pick, cells_v, cells_s, wide_a, wide_b, yhi, ylo, zt, out, sems) = scratch[
+    gain, thi, tlo, pick, cells_v, cells_s, wide_a, wide_b, yhi, ylo, zt, out, sems = scratch[
         STREAMS:
     ]
-    groups, capacity, _ = recv.shape
+    groups, rows_in, _ = recv.shape
+    capacity = rows_in - SUB
     lat_dev = gain.shape[0]
     blocks = gain.shape[2] // LANES
-    first = pltpu.make_async_copy(recv_hbm.at[:, pl.ds(capacity, SUB)], extra, sems.at[0])
-    first.start()
-    parts = 4
-    each = groups // parts
-    deps = [
-        pltpu.make_async_copy(
-            recv_hbm.at[pl.ds(i * each, each), pl.ds(0, capacity)],
-            recv.at[pl.ds(i * each, each)],
-            sems.at[2 + i],
-        )
-        for i in range(parts)
-    ]
     half = lat_dev // 2
     loads = [
-        pltpu.make_async_copy(src, dst, sems.at[2 + parts + i])
+        pltpu.make_async_copy(src, dst, sems.at[1 + i])
         for i, (src, dst) in enumerate(
             (
                 (gain_hbm.at[pl.ds(0, half)], gain.at[pl.ds(0, half)]),
@@ -197,8 +196,12 @@
             )
         )
     ]
-    for copy in deps:
+    for copy in loads:
         copy.start()
+
+    cells_v[...] = recv[:, capacity, :].astype(I32)
+    cell_copy = pltpu.make_async_copy(cells_v, cells_s, sems.at[0])
+    cell_copy.start()
 
     def clear(i, carry):
         for a in acc:
@@ -207,13 +210,9 @@
 
     lax.fori_loop(0, acc[0].shape[0] // SUB, clear, 0)
 
-    first.wait()
-    cells_v[...] = extra[:, 0, :].astype(I32)
-    cell_copy = pltpu.make_async_copy(cells_v, cells_s, sems.at[1])
-    cell_copy.start()
 
     rows = groups * SUB
-    weight = extra[...].reshape(rows, LANES)
+    weight = recv[:, capacity:, :].reshape(rows, LANES)
     lane = lax.broadcasted_iota(I32, (rows, LANES), 1)
     whi, wlo = split(weight)
     both = jnp.where(
@@ -242,10 +241,6 @@
 
     widen(wide_a, 0)
     cell_copy.wait()
-    for copy in deps:
-        copy.wait()
-    for copy in loads:
-        copy.start()
 
     def scatter(i, carry):
         k0 = 4 * i
@@ -331,7 +326,7 @@
                 ]
         span = pl.ds(j0 * chunks, tall * chunks)
         sends.append(
-            pltpu.make_async_copy(out.at[span], out_hbm.at[span], sems.at[11 + j0 // tall])
+            pltpu.make_async_copy(out.at[span], out_hbm.at[span], sems.at[6 + j0 // tall])
         )
         sends[-1].start()
     for copy in sends:
@@ -347,12 +342,11 @@
     return pl.pallas_call(
         grid_kernel,
         out_shape=jax.ShapeDtypeStruct((waves * 2 * rows // LANES, LANES), F32),
-        in_specs=[pl.BlockSpec(memory_space=pltpu.HBM)] * 5,
+        in_specs=[pl.BlockSpec(memory_space=pltpu.VMEM)]
+        + [pl.BlockSpec(memory_space=pltpu.HBM)] * 4,
         out_specs=pl.BlockSpec(memory_space=pltpu.HBM),
         scratch_shapes=[pltpu.VMEM((cells, ch_dev, LANES), F32) for _ in range(STREAMS)]
         + [
-            pltpu.VMEM((groups, capacity, LANES), F32),
-            pltpu.VMEM((groups, SUB, LANES), F32),
             pltpu.VMEM(gain.shape, F32),
             pltpu.VMEM(thi.shape, BF16),
             pltpu.VMEM(tlo.shape, BF16),
@@ -365,7 +359,7 @@
             pltpu.VMEM((GROUPS, rows, thi.shape[1]), BF16),
             pltpu.VMEM((2 * waves, 2 * rows), BF16),
             pltpu.VMEM((waves * 2 * rows // LANES, LANES), F32),
-            pltpu.SemaphoreType.DMA((11 + waves // LANES,)),
+            pltpu.SemaphoreType.DMA((6 + waves // LANES,)),
         ],
         compiler_params=pltpu.CompilerParams(vmem_limit_bytes=52 * MIB),
         name="grid_to_waves",
@@ -422,27 +416,23 @@
     )(band_of, legendre)
 
 
-def legendre_kernel(geo, x_hbm, lhi_hbm, llo_hbm, out_hbm, x_ref, lhi, llo, out, sems):
+def legendre_kernel(geo, x_ref, lhi_hbm, llo_hbm, out_hbm, lhi, llo, out, sems):
     grid_count, lev_count, slot_count, chunks = geo
     full = LANES // grid_count
     wide = 2 * SUB
-    first = pltpu.make_async_copy(x_hbm, x_ref, sems.at[0])
-    first.start()
-
     def loads(slot):
         return [
-            pltpu.make_async_copy(src.at[slot], dst.at[slot], sems.at[1 + 2 * slot + i])
+            pltpu.make_async_copy(src.at[slot], dst.at[slot], sems.at[2 * slot + i])
             for i, (src, dst) in enumerate(((lhi_hbm, lhi), (llo_hbm, llo)))
         ]
 
     for slot in range(AHEAD):
         for copy in loads(slot):
             copy.start()
-    first.wait()
 
     def store(slot):
         return pltpu.make_async_copy(
-            out.at[slot], out_hbm.at[slot], sems.at[1 + 2 * slot_count + slot]
+            out.at[slot], out_hbm.at[slot], sems.at[2 * slot_count + slot]
         )
 
     def body(slot, carry):
@@ -496,14 +486,14 @@
     return pl.pallas_call(
         functools.partial(legendre_kernel, geo),
         out_shape=jax.ShapeDtypeStruct(out_shape, F32),
-        in_specs=[pl.BlockSpec(memory_space=pltpu.HBM)] * 3,
+        in_specs=[pl.BlockSpec(memory_space=pltpu.VMEM)]
+        + [pl.BlockSpec(memory_space=pltpu.HBM)] * 2,
         out_specs=pl.BlockSpec(memory_space=pltpu.HBM),
         scratch_shapes=[
-            pltpu.VMEM(waves.shape, F32),
             pltpu.VMEM(lhi.shape, BF16),
             pltpu.VMEM(llo.shape, BF16),
             pltpu.VMEM(out_shape, F32),
-            pltpu.SemaphoreType.DMA((1 + 3 * slot_count,)),
+            pltpu.SemaphoreType.DMA((3 * slot_count,)),
         ],
         compiler_params=pltpu.CompilerParams(vmem_limit_bytes=50 * MIB),
         name="legendre_step",

time: 84.2 us -> 83.1 us (0.987)
  Pallas kernels: 40 us -> 38.9 us
where the time goes in v2:
time: 83.1 us; the launch traced here: 82.6 us
  Pallas kernels  38.9 us (47%)
  waiting for transfers between devices  18.3 us (22%)
  starting transfers between devices  16.1 us (19%)
  other arithmetic  9.3 us (11%)
    pallas_call x1, Pallas kernels, prepare_table(): pl.pallas_call(functools.partial(prepare_kernel, lat_dev), grid=(slot_cou...  15.8 us
    pallas_call x1, Pallas kernels, grid_to_waves(): pl.pallas_call(grid_kernel, out_shape=jax.ShapeDtypeStruct((waves * 2 * r...  13.5 us
    all_to_all x1, waiting for transfers between devices, shards(): lax.all_to_all(outgoing, ('grid', 'lev'), split_axis=0, concat_axis=0, ti...  9.88 us
    all_to_all x1, starting transfers between devices, shards(): recv = lax.all_to_all(sent, 'grid', split_axis=0, concat_axis=0, tiled=True)  8.6 us
    transpose x1, other arithmetic, shards(): gain = jnp.swapaxes(1.0 + 0.5 * jnp.tanh(trajectory), 0, 1)  8.39 us
    all_to_all x1, waiting for transfers between devices, shards(): recv = lax.all_to_all(sent, 'grid', split_axis=0, concat_axis=0, tiled=True)  8.38 us
    pallas_call x1, Pallas kernels, legendre_step(): pl.pallas_call(functools.partial(legendre_kernel, geo), out_shape=jax.Sha...  7.53 us
    all_to_all x1, starting transfers between devices, shards(): lax.all_to_all(outgoing, ('grid', 'lev'), split_axis=0, concat_axis=0, ti...  7.53 us
  transfers between devices with their start and end apart: 2, of which 2 were waited for; matrix products, arithmetic and copies ran while one was open for 11% of the time, Pallas kernels for 19%

profile of v2, /device:TPU:1, one launch (start us, length us, event | category | flops | bytes accessed | tf_op | source)
XLA Modules:
  0.0 82.6 jit_solution(11106921458125605666)
XLA Ops:
  0.0 2.1 %pack.1 = f32[32,72,128]{2,1,0:T(8,128)} custom-call(s32[32]{0:T(128)} %count_hbm.1, f32[32,64,128]{2,1,0:T(8,128)} %bitcast.8, f32[8,2048]{1,0:T(8,128)} %weight_hbm.1, s32[16,128]{1,0:T(8,128)} %bitcast.9), custom_call_target="tpu_custom_call" | custom-call | tf_op jit(solution)/shard_map/pack/pallas_call | solution.py:154
  2.1 8.6 %all-to-all-start = ((f32[32,72,128]{2,1,0:T(8,128)}), f32[32,72,128]{2,1,0:T(8,128)S(1)}, u32[]{:S(2)}, u32[]{:S(2)}) async-start(f32[32,72,128]{2,1,0:T(8,128)} %pack.1), calls=%async_computation | async-start | bytes 2359296 | tf_op jit(solution)/shard_map/all_to_all | solution.py:512
  10.7 0.9 %compare_convert_fusion.pick_hbm = bf16[640,640]{1,0:T(8,128)(2,1)S(1)} fusion(s32[640]{0:T(1024)} %constant.15, s32[640]{0:T(1024)} %param.18), kind=kLoop, calls=%fused_computation.4 | loop fusion | flops 819200 | bytes 824320 | tf_op jit(solution)/shard_map/convert_element_type | solution.py:517
  11.7 8.4 %fusion.2.gain_hbm = f32[40,8,4096]{2,1,0:T(8,128)} fusion(f32[8,40,4096]{2,1,0:T(8,128)} %param.11), kind=kLoop, calls=%fused_computation.3 | loop fusion | flops 2621440 | bytes 10485760 | tf_op jit(solution)/shard_map/transpose | solution.py:514
  20.1 8.4 %all-to-all-done.recv = f32[32,72,128]{2,1,0:T(8,128)S(1)} async-done(((f32[32,72,128]{2,1,0:T(8,128)}), f32[32,72,128]{2,1,0:T(8,128)S(1)}, u32[]{:S(2)}, u32[]{:S(2)}) %all-to-all-start) | async-done | bytes 1179680 | tf_op jit(solution)/shard_map/all_to_all | solution.py:512
  28.4 13.5 %grid_to_waves.1 = f32[3200,128]{1,0:T(8,128)} custom-call(f32[32,72,128]{2,1,0:T(8,128)S(1)} %all-to-all-done.recv, f32[40,8,4096]{2,1,0:T(8,128)} %fusion.2.gain_hbm, bf16[8,512,256]{2,1,0:T(8,128)(2,1)} %constant.11.clone.thi_hbm, bf16[8,512,256]{2,1,0:T(8,128)(2,1)} %constant.12.clone.tlo_hbm, bf16[640,640]{1,0:T(8,128)(2,1)S(1)} %compare_convert_fusion.pick_hbm), custom_call_target="tpu_custom_call" | custom-call | tf_op jit(solution)/shard_map/grid_to_waves/pallas_call | solution.py:342
  41.9 7.5 %all-to-all-start.1 = ((f32[128,1,3200]{2,1,0:T(1,128)}), f32[128,1,3200]{2,1,0:T(1,128)S(1)}, u32[]{:S(2)}, u32[]{:S(2)}) async-start(f32[128,1,3200]{2,1,0:T(1,128)} %bitcast.7), calls=%async_computation.1 | async-start | bytes 3276800 | tf_op jit(solution)/shard_map/all_to_all | solution.py:521
  49.5 15.8 %prepare_table.1 = (bf16[5,1280,640]{2,1,0:T(8,128)(2,1)}, bf16[5,1280,640]{2,1,0:T(8,128)(2,1)}) custom-call(s32[32]{0:T(128)} %band_ref.1, f32[5,1280,640]{2,1,0:T(8,128)} %table_ref.1), custom_call_target="tpu_custom_call" | custom-call | flops 16384000 | bytes 32768000 | tf_op jit(solution)/shard_map/prepare_table/pallas_call | solution.py:405
  65.2 9.9 %all-to-all-done.1 = f32[128,1,3200]{2,1,0:T(1,128)S(1)} async-done(((f32[128,1,3200]{2,1,0:T(1,128)}), f32[128,1,3200]{2,1,0:T(1,128)S(1)}, u32[]{:S(2)}, u32[]{:S(2)}) %all-to-all-start.1) | async-done | bytes 1638432 | tf_op jit(solution)/shard_map/all_to_all | solution.py:521
  75.1 7.5 %legendre_step.1 = f32[5,32,2,640]{3,2,1,0:T(2,128)} custom-call(f32[3200,128]{1,0:T(8,128)S(1)} %bitcast.6, bf16[5,1280,640]{2,1,0:T(8,128)(2,1)} %get-tuple-element.7.lhi_hbm, bf16[5,1280,640]{2,1,0:T(8,128)(2,1)} %get-tuple-element.8.llo_hbm), custom_call_target="tpu_custom_call" | custom-call | tf_op jit(solution)/shard_map/legendre_step/pallas_call | solution.py:486
Async XLA Ops:
  2.1 26.3 %all-to-all-start = ((f32[32,72,128]{2,1,0:T(8,128)}), f32[32,72,128]{2,1,0:T(8,128)S(1)}, u32[]{:S(2)}, u32[]{:S(2)}) async-start(f32[32,72,128]{2,1,0:T(8,128)} %pack.1), calls=%async_computation | async-start | bytes 2359296 | tf_op jit(solution)/shard_map/all_to_all | solution.py:512
  41.9 33.2 %all-to-all-start.1 = ((f32[128,1,3200]{2,1,0:T(1,128)}), f32[128,1,3200]{2,1,0:T(1,128)S(1)}, u32[]{:S(2)}, u32[]{:S(2)}) async-start(f32[128,1,3200]{2,1,0:T(1,128)} %bitcast.7), calls=%async_computation.1 | async-start | bytes 3276800 | tf_op jit(solution)/shard_map/all_to_all | solution.py:521
